TPU v7x, 128 devices: a whole 4x4x4 slice. The times are simulated.
128 devices in a mesh: grp: 8 (over x, core), tile: 16 (over y, z).
Axes of the slice: x: 4, y: 4, z: 4, core: 2. Of those that a mesh axis runs over, the one named last changes fastest.
Arguments:
- molecule_coords: float32 [3, 2097152], P(None, ('grp', 'tile')), may hold values from 0 to 1.6
- molecule_speeds: float32 [3, 2097152], P(None, ('grp', 'tile')), may hold values from -6 to 6
- molecule_thermal_state: float32 [2097152], P(('grp', 'tile')), may hold values from 0.5 to 2
- conservative_strength: float32 [2097152], P(('grp', 'tile')), may hold values from 0.05 to 0.5
- noise_keys: int32 [2097152], P(('grp', 'tile')), may hold values from 0 to 32767
- exported_tile_places: int32 [128, 16, 12], P(('grp', 'tile')), may hold values from 0 to 127
- tile_couplings: int32 [128, 1024, 2], P(('grp', 'tile')), may hold values from 0 to 383, as said below
- processor_coupling_tally: int32 [128], P(('grp', 'tile')), may hold values from 512 to 1024
Outputs:
- force_heat: float32 [4, 2097152], P(None, ('grp', 'tile'))
Inputs may be any that keep to these rules, and one draw needn't show every extreme that they name: `tile_couplings`: second slots of workers in the lowest slab are below 192; first slots are below 192.
All inputs are finite; a program needn't handle non-finite values.
Results may differ from a plain program's by a relative error of at most 0.0003.
Values sent between devices are 32-bit elements; how exact they have to be, the bound alone decides.
A program may use at most 128 MiB of HBM per device.

v0:
```python
import math
import jax
import jax.numpy as jnp
from jax import lax
from jax.sharding import PartitionSpec as P

friction = 0.45
noise_amp = 0.3
conductivity = 0.1


def passed_along(value, axis, steps):
    count = lax.axis_size(axis)
    leading, last = (max(0, -steps), min(count, count - steps))
    return lax.ppermute(value, axis, [(source, source + steps) for source in range(leading, last)])


def tile_pair(first, second):
    offset = first[0:3, :, None] - second[0:3, None, :]
    radius = jnp.sqrt(jnp.sum(offset * offset, 0) + 0.01)
    unit = offset / radius
    weight = jnp.maximum(1.0 - radius, 0.0)
    relative = first[3:6, :, None] - second[3:6, None, :]
    along = jnp.sum(unit * relative, 0)
    repulse = 0.5 * (first[7][:, None] + second[7][None, :])
    seed_first = first[8].astype(jnp.int32)
    seed_second = second[8].astype(jnp.int32)
    hashed = (
        seed_first[:, None] * seed_second[None, :] + seed_first[:, None] + seed_second[None, :]
    ) % 65521
    noise = hashed.astype(jnp.float32) * (2.0 / 65521.0) - 1.0
    magnitude = repulse * weight - friction * weight * weight * along + noise_amp * weight * noise
    force = magnitude[None] * unit
    conduct = conductivity * weight * weight * (second[6][None, :] - first[6][:, None])
    viscous = 0.5 * friction * weight * weight * along * along
    on_first = jnp.concatenate([jnp.sum(force, 2), jnp.sum(conduct + viscous, 1)[None]], 0)
    on_second = jnp.concatenate([-jnp.sum(force, 1), jnp.sum(viscous - conduct, 0)[None]], 0)
    return (on_first, on_second)


def tile_self(block_data):
    offset = block_data[0:3, :, None] - block_data[0:3, None, :]
    radius = jnp.sqrt(jnp.sum(offset * offset, 0) + 0.01)
    unit = offset / radius
    weight = jnp.maximum(1.0 - radius, 0.0)
    relative = block_data[3:6, :, None] - block_data[3:6, None, :]
    along = jnp.sum(unit * relative, 0)
    repulse = 0.5 * (block_data[7][:, None] + block_data[7][None, :])
    seed_first = block_data[8].astype(jnp.int32)
    hashed = (
        seed_first[:, None] * seed_first[None, :] + seed_first[:, None] + seed_first[None, :]
    ) % 65521
    noise = hashed.astype(jnp.float32) * (2.0 / 65521.0) - 1.0
    others = 1.0 - jnp.eye(block_data.shape[1], dtype=jnp.float32)
    magnitude = (
        repulse * weight - friction * weight * weight * along + noise_amp * weight * noise
    ) * others
    force = magnitude[None] * unit
    conduct = conductivity * weight * weight * (block_data[6][None, :] - block_data[6][:, None])
    viscous = 0.5 * friction * weight * weight * along * along
    heating = jnp.sum((conduct + viscous) * others, 1)
    return jnp.concatenate([jnp.sum(force, 2), heating[None]], 0)


def one_hot(indices, count):
    return (indices[:, None] == jnp.arange(count, dtype=jnp.int32)[None, :]).astype(jnp.float32)


def per_device(
    molecule_coords,
    molecule_speeds,
    molecule_thermal_state,
    conservative_strength,
    noise_keys,
    exported_tile_places,
    tile_couplings,
    processor_coupling_tally,
):
    n_tile = lax.axis_size("tile")
    blocks = molecule_coords.shape[1] // 128
    slot_table = exported_tile_places[0]
    cap = slot_table.shape[1]
    buffer_len = n_tile * cap
    owned = jnp.concatenate(
        [
            molecule_coords,
            molecule_speeds,
            molecule_thermal_state[None],
            conservative_strength[None],
            noise_keys[None].astype(jnp.float32),
        ],
        0,
    )
    owned = owned.reshape(9, blocks, 128).transpose(1, 0, 2)
    group_data = lax.all_gather(owned, "tile", axis=0, tiled=True)
    tables = lax.all_gather(exported_tile_places, "tile", axis=0, tiled=True)
    my_index = lax.axis_index("tile")
    my_slots = lax.dynamic_index_in_dim(tables, my_index, 1, keepdims=False)
    group_ids = (jnp.arange(n_tile, dtype=jnp.int32)[:, None] * blocks + my_slots).reshape(-1)
    held_blocks = group_data[group_ids]
    neighbour = passed_along(held_blocks, "grp", 1)
    reachable = jnp.concatenate([held_blocks, neighbour], 0)
    total_pair_count = tile_couplings.shape[1]
    batch = math.gcd(total_pair_count, 64)
    first_slots = tile_couplings[0, :, 0].reshape(-1, batch)
    second_slots = tile_couplings[0, :, 1].reshape(-1, batch)
    live_rows = (
        (jnp.arange(total_pair_count, dtype=jnp.int32) < processor_coupling_tally[0])
        .astype(jnp.float32)
        .reshape(-1, batch)
    )

    def consume(carry, items):
        near_acc, far_acc = carry
        first_idx, second_index, live = items
        on_first, on_second = jax.vmap(tile_pair)(held_blocks[first_idx], reachable[second_index])
        on_first = (on_first * live[:, None, None]).reshape(batch, 512)
        on_second = (on_second * live[:, None, None]).reshape(batch, 512)
        near_acc = near_acc + jnp.dot(
            one_hot(first_idx, buffer_len).T, on_first, precision=lax.Precision.HIGHEST
        )
        far_acc = far_acc + jnp.dot(
            one_hot(second_index, 2 * buffer_len).T, on_second, precision=lax.Precision.HIGHEST
        )
        return ((near_acc, far_acc), None)

    start_carry = (
        jnp.zeros((buffer_len, 512), jnp.float32),
        jnp.zeros((2 * buffer_len, 512), jnp.float32),
    )
    (near_acc, far_acc), _ = lax.scan(consume, start_carry, (first_slots, second_slots, live_rows))
    lower_terms = passed_along(far_acc[buffer_len:], "grp", -1)
    own_total = near_acc + far_acc[:buffer_len] + lower_terms
    selector = one_hot(group_ids, n_tile * blocks)
    summed = lax.psum_scatter(
        jnp.dot(selector.T, own_total, precision=lax.Precision.HIGHEST),
        "tile",
        scatter_dimension=0,
        tiled=True,
    )
    self_batch = math.gcd(blocks, 16)

    def self_step(carry, group_data):
        return (carry, jax.vmap(tile_self)(group_data))

    _, selfs = lax.scan(
        self_step, jnp.zeros((), jnp.float32), owned.reshape(-1, self_batch, 9, 128)
    )
    result = summed.reshape(blocks, 4, 128) + selfs.reshape(blocks, 4, 128)
    return result.transpose(1, 0, 2).reshape(4, blocks * 128)


def solution(mesh):
    in_specs = (
        P(None, ("grp", "tile")),
        P(None, ("grp", "tile")),
        P(("grp", "tile")),
        P(("grp", "tile")),
        P(("grp", "tile")),
        P(("grp", "tile"), None, None),
        P(("grp", "tile"), None, None),
        P(("grp", "tile")),
    )
    out_specs = P(None, ("grp", "tile"))
    return jax.shard_map(
        per_device, mesh=mesh, in_specs=in_specs, out_specs=out_specs, check_vma=False
    )
```

profile of v0, /device:TPU:0, one launch (start us, length us, event | category | flops | bytes accessed | tf_op | source)
XLA Modules:
  0.0 833.5 jit_solution(1761941762387604038)
XLA Ops:
  12.7 25.4 %all_gather.6 = s32[16,16,12]{2,1,0:T(8,128)S(1)} all-gather(s32[1,16,12]{2,1,0:T(8,128)S(1)} %copy.32), channel_id=1, replica_groups=mesh['grp'=8,'tile'=16] {'tile'}, dimensions={0}, use_global_device_ids=true | all-gather | bytes 13056 | tf_op jit(solution)/shard_map/all_gather | solution.py:96
  40.1 50.3 %all-gather.2.cloned.1.call-done = f32[2048,9,128]{2,0,1:T(8,128)} async-done(((f32[128,9,128]{2,0,1:T(8,128)}), f32[2048,9,128]{2,0,1:T(8,128)}) %all-gather.2.cloned.1.call-update) | async-done | bytes 9437200 | tf_op jit(solution)/shard_map/all_gather | solution.py:95
  90.5 12.8 %copy.33 = f32[2048,9,128]{2,1,0:T(8,128)} copy(f32[2048,9,128]{2,0,1:T(8,128)} %all-gather.2.cloned.1.call-done) | data formatting | bytes 18874368 | tf_op jit(solution)/shard_map/all_gather | solution.py:95
  103.2 6.5 gather_fusion.2
  117.3 606.1 %while.28 = (s32[]{:T(128)}, f32[192,512]{1,0:T(8,128)}, f32[384,512]{1,0:T(8,128)S(1)}, s32[16,64]{1,0:T(8,128)S(1)}, f32[192,9,128]{2,1,0:T(8,128)S(1)}, /*ind...) while((s32[]{:T(128)}, f32[192,512]{1,0:T(8,128)}, ...), condition=%wide.region_7.8_spmd.clone, body=%wide.region_0.7_spmd.clone.sunk | while | flops 305871232 | bytes 52507452 | solution.py:131
  121.3 4.1 fusion.72
  126.5 8.0 multiply_reduce_fusion.11
  134.7 9.2 %subtract_reduce_fusion.2 = (f32[64,128]{1,0:T(8,128)S(1)}, f32[64,128]{1,0:T(8,128)S(1)}, f32[64,128,128]{2,1,0:T(8,128)S(1)}) fusion(f32[64,128,128]{2,1,0:T(8,128)S(1)} %multiply_reduce_fusion.11, f32[64,128]{1,0:T(8,128)S(1)} %bitcast.118, f32[64,128]{1,0:T(8,128)S(1)} %bitcast.115, f32[64,128,128]{2,1,0:T(8,128)S(1)} %fusion.72, ...), kind=kLoop, calls=%fused_computation.59.clone.1 | loop fusion | flops 38780928 | bytes 12845056 | tf_op jit(solution)/shard_map/while/body/eval_jaxpr/vmap()/reduce_sum | solution.py:37
  143.9 8.5 %multiply_reduce_fusion.12 = (f32[64,3,128]{2,1,0:T(4,128)S(1)}, f32[64,3,128]{2,1,0:T(4,128)S(1)}) fusion(f32[64,128,128]{2,1,0:T(8,128)S(1)} %get-tuple-element.365, f32[64,128,128]{2,1,0:T(8,128)S(1)} %add_sqrt_fusion.5, f32[64,3,128]{2,1,0:T(4,128)S(1)} %get-tuple-element.356, f32[64,3,128]{2,1,0:T(4,128)S(1)} %get-tuple-element.357), kind=kLoop, calls=%fused_computation.44.clone.1 | loop fusion | flops 15679488 | bytes 8781824 | tf_op jit(solution)/shard_map/while/body/eval_jaxpr/vmap()/reduce_sum | solution.py:37
  159.1 4.1 fusion.72
  164.4 8.0 multiply_reduce_fusion.11
  172.6 9.2 %subtract_reduce_fusion.2 = (f32[64,128]{1,0:T(8,128)S(1)}, f32[64,128]{1,0:T(8,128)S(1)}, f32[64,128,128]{2,1,0:T(8,128)S(1)}) fusion(f32[64,128,128]{2,1,0:T(8,128)S(1)} %multiply_reduce_fusion.11, f32[64,128]{1,0:T(8,128)S(1)} %bitcast.118, f32[64,128]{1,0:T(8,128)S(1)} %bitcast.115, f32[64,128,128]{2,1,0:T(8,128)S(1)} %fusion.72, ...), kind=kLoop, calls=%fused_computation.59.clone.1 | loop fusion | flops 38780928 | bytes 12845056 | tf_op jit(solution)/shard_map/while/body/eval_jaxpr/vmap()/reduce_sum | solution.py:37
  181.8 8.5 %multiply_reduce_fusion.12 = (f32[64,3,128]{2,1,0:T(4,128)S(1)}, f32[64,3,128]{2,1,0:T(4,128)S(1)}) fusion(f32[64,128,128]{2,1,0:T(8,128)S(1)} %get-tuple-element.365, f32[64,128,128]{2,1,0:T(8,128)S(1)} %add_sqrt_fusion.5, f32[64,3,128]{2,1,0:T(4,128)S(1)} %get-tuple-element.356, f32[64,3,128]{2,1,0:T(4,128)S(1)} %get-tuple-element.357), kind=kLoop, calls=%fused_computation.44.clone.1 | loop fusion | flops 15679488 | bytes 8781824 | tf_op jit(solution)/shard_map/while/body/eval_jaxpr/vmap()/reduce_sum | solution.py:37
  202.3 8.0 multiply_reduce_fusion.11
  210.4 9.2 %subtract_reduce_fusion.2 = (f32[64,128]{1,0:T(8,128)S(1)}, f32[64,128]{1,0:T(8,128)S(1)}, f32[64,128,128]{2,1,0:T(8,128)S(1)}) fusion(f32[64,128,128]{2,1,0:T(8,128)S(1)} %multiply_reduce_fusion.11, f32[64,128]{1,0:T(8,128)S(1)} %bitcast.118, f32[64,128]{1,0:T(8,128)S(1)} %bitcast.115, f32[64,128,128]{2,1,0:T(8,128)S(1)} %fusion.72, ...), kind=kLoop, calls=%fused_computation.59.clone.1 | loop fusion | flops 38780928 | bytes 12845056 | tf_op jit(solution)/shard_map/while/body/eval_jaxpr/vmap()/reduce_sum | solution.py:37
  219.7 8.5 %multiply_reduce_fusion.12 = (f32[64,3,128]{2,1,0:T(4,128)S(1)}, f32[64,3,128]{2,1,0:T(4,128)S(1)}) fusion(f32[64,128,128]{2,1,0:T(8,128)S(1)} %get-tuple-element.365, f32[64,128,128]{2,1,0:T(8,128)S(1)} %add_sqrt_fusion.5, f32[64,3,128]{2,1,0:T(4,128)S(1)} %get-tuple-element.356, f32[64,3,128]{2,1,0:T(4,128)S(1)} %get-tuple-element.357), kind=kLoop, calls=%fused_computation.44.clone.1 | loop fusion | flops 15679488 | bytes 8781824 | tf_op jit(solution)/shard_map/while/body/eval_jaxpr/vmap()/reduce_sum | solution.py:37
  240.2 8.0 multiply_reduce_fusion.11
  248.3 9.2 %subtract_reduce_fusion.2 = (f32[64,128]{1,0:T(8,128)S(1)}, f32[64,128]{1,0:T(8,128)S(1)}, f32[64,128,128]{2,1,0:T(8,128)S(1)}) fusion(f32[64,128,128]{2,1,0:T(8,128)S(1)} %multiply_reduce_fusion.11, f32[64,128]{1,0:T(8,128)S(1)} %bitcast.118, f32[64,128]{1,0:T(8,128)S(1)} %bitcast.115, f32[64,128,128]{2,1,0:T(8,128)S(1)} %fusion.72, ...), kind=kLoop, calls=%fused_computation.59.clone.1 | loop fusion | flops 38780928 | bytes 12845056 | tf_op jit(solution)/shard_map/while/body/eval_jaxpr/vmap()/reduce_sum | solution.py:37
  257.5 8.5 %multiply_reduce_fusion.12 = (f32[64,3,128]{2,1,0:T(4,128)S(1)}, f32[64,3,128]{2,1,0:T(4,128)S(1)}) fusion(f32[64,128,128]{2,1,0:T(8,128)S(1)} %get-tuple-element.365, f32[64,128,128]{2,1,0:T(8,128)S(1)} %add_sqrt_fusion.5, f32[64,3,128]{2,1,0:T(4,128)S(1)} %get-tuple-element.356, f32[64,3,128]{2,1,0:T(4,128)S(1)} %get-tuple-element.357), kind=kLoop, calls=%fused_computation.44.clone.1 | loop fusion | flops 15679488 | bytes 8781824 | tf_op jit(solution)/shard_map/while/body/eval_jaxpr/vmap()/reduce_sum | solution.py:37
  278.0 8.0 multiply_reduce_fusion.11
  286.2 9.2 %subtract_reduce_fusion.2 = (f32[64,128]{1,0:T(8,128)S(1)}, f32[64,128]{1,0:T(8,128)S(1)}, f32[64,128,128]{2,1,0:T(8,128)S(1)}) fusion(f32[64,128,128]{2,1,0:T(8,128)S(1)} %multiply_reduce_fusion.11, f32[64,128]{1,0:T(8,128)S(1)} %bitcast.118, f32[64,128]{1,0:T(8,128)S(1)} %bitcast.115, f32[64,128,128]{2,1,0:T(8,128)S(1)} %fusion.72, ...), kind=kLoop, calls=%fused_computation.59.clone.1 | loop fusion | flops 38780928 | bytes 12845056 | tf_op jit(solution)/shard_map/while/body/eval_jaxpr/vmap()/reduce_sum | solution.py:37
  295.4 8.5 %multiply_reduce_fusion.12 = (f32[64,3,128]{2,1,0:T(4,128)S(1)}, f32[64,3,128]{2,1,0:T(4,128)S(1)}) fusion(f32[64,128,128]{2,1,0:T(8,128)S(1)} %get-tuple-element.365, f32[64,128,128]{2,1,0:T(8,128)S(1)} %add_sqrt_fusion.5, f32[64,3,128]{2,1,0:T(4,128)S(1)} %get-tuple-element.356, f32[64,3,128]{2,1,0:T(4,128)S(1)} %get-tuple-element.357), kind=kLoop, calls=%fused_computation.44.clone.1 | loop fusion | flops 15679488 | bytes 8781824 | tf_op jit(solution)/shard_map/while/body/eval_jaxpr/vmap()/reduce_sum | solution.py:37
  310.7 4.1 fusion.72
  315.9 8.0 multiply_reduce_fusion.11
  324.1 9.2 %subtract_reduce_fusion.2 = (f32[64,128]{1,0:T(8,128)S(1)}, f32[64,128]{1,0:T(8,128)S(1)}, f32[64,128,128]{2,1,0:T(8,128)S(1)}) fusion(f32[64,128,128]{2,1,0:T(8,128)S(1)} %multiply_reduce_fusion.11, f32[64,128]{1,0:T(8,128)S(1)} %bitcast.118, f32[64,128]{1,0:T(8,128)S(1)} %bitcast.115, f32[64,128,128]{2,1,0:T(8,128)S(1)} %fusion.72, ...), kind=kLoop, calls=%fused_computation.59.clone.1 | loop fusion | flops 38780928 | bytes 12845056 | tf_op jit(solution)/shard_map/while/body/eval_jaxpr/vmap()/reduce_sum | solution.py:37
  333.3 8.5 %multiply_reduce_fusion.12 = (f32[64,3,128]{2,1,0:T(4,128)S(1)}, f32[64,3,128]{2,1,0:T(4,128)S(1)}) fusion(f32[64,128,128]{2,1,0:T(8,128)S(1)} %get-tuple-element.365, f32[64,128,128]{2,1,0:T(8,128)S(1)} %add_sqrt_fusion.5, f32[64,3,128]{2,1,0:T(4,128)S(1)} %get-tuple-element.356, f32[64,3,128]{2,1,0:T(4,128)S(1)} %get-tuple-element.357), kind=kLoop, calls=%fused_computation.44.clone.1 | loop fusion | flops 15679488 | bytes 8781824 | tf_op jit(solution)/shard_map/while/body/eval_jaxpr/vmap()/reduce_sum | solution.py:37
  353.8 8.0 multiply_reduce_fusion.11
  362.0 9.2 %subtract_reduce_fusion.2 = (f32[64,128]{1,0:T(8,128)S(1)}, f32[64,128]{1,0:T(8,128)S(1)}, f32[64,128,128]{2,1,0:T(8,128)S(1)}) fusion(f32[64,128,128]{2,1,0:T(8,128)S(1)} %multiply_reduce_fusion.11, f32[64,128]{1,0:T(8,128)S(1)} %bitcast.118, f32[64,128]{1,0:T(8,128)S(1)} %bitcast.115, f32[64,128,128]{2,1,0:T(8,128)S(1)} %fusion.72, ...), kind=kLoop, calls=%fused_computation.59.clone.1 | loop fusion | flops 38780928 | bytes 12845056 | tf_op jit(solution)/shard_map/while/body/eval_jaxpr/vmap()/reduce_sum | solution.py:37
  371.2 8.5 %multiply_reduce_fusion.12 = (f32[64,3,128]{2,1,0:T(4,128)S(1)}, f32[64,3,128]{2,1,0:T(4,128)S(1)}) fusion(f32[64,128,128]{2,1,0:T(8,128)S(1)} %get-tuple-element.365, f32[64,128,128]{2,1,0:T(8,128)S(1)} %add_sqrt_fusion.5, f32[64,3,128]{2,1,0:T(4,128)S(1)} %get-tuple-element.356, f32[64,3,128]{2,1,0:T(4,128)S(1)} %get-tuple-element.357), kind=kLoop, calls=%fused_computation.44.clone.1 | loop fusion | flops 15679488 | bytes 8781824 | tf_op jit(solution)/shard_map/while/body/eval_jaxpr/vmap()/reduce_sum | solution.py:37
  391.7 8.0 multiply_reduce_fusion.11
  399.9 9.2 %subtract_reduce_fusion.2 = (f32[64,128]{1,0:T(8,128)S(1)}, f32[64,128]{1,0:T(8,128)S(1)}, f32[64,128,128]{2,1,0:T(8,128)S(1)}) fusion(f32[64,128,128]{2,1,0:T(8,128)S(1)} %multiply_reduce_fusion.11, f32[64,128]{1,0:T(8,128)S(1)} %bitcast.118, f32[64,128]{1,0:T(8,128)S(1)} %bitcast.115, f32[64,128,128]{2,1,0:T(8,128)S(1)} %fusion.72, ...), kind=kLoop, calls=%fused_computation.59.clone.1 | loop fusion | flops 38780928 | bytes 12845056 | tf_op jit(solution)/shard_map/while/body/eval_jaxpr/vmap()/reduce_sum | solution.py:37
  409.1 8.5 %multiply_reduce_fusion.12 = (f32[64,3,128]{2,1,0:T(4,128)S(1)}, f32[64,3,128]{2,1,0:T(4,128)S(1)}) fusion(f32[64,128,128]{2,1,0:T(8,128)S(1)} %get-tuple-element.365, f32[64,128,128]{2,1,0:T(8,128)S(1)} %add_sqrt_fusion.5, f32[64,3,128]{2,1,0:T(4,128)S(1)} %get-tuple-element.356, f32[64,3,128]{2,1,0:T(4,128)S(1)} %get-tuple-element.357), kind=kLoop, calls=%fused_computation.44.clone.1 | loop fusion | flops 15679488 | bytes 8781824 | tf_op jit(solution)/shard_map/while/body/eval_jaxpr/vmap()/reduce_sum | solution.py:37
  424.3 4.1 fusion.72
  429.6 8.0 multiply_reduce_fusion.11
  437.7 9.2 %subtract_reduce_fusion.2 = (f32[64,128]{1,0:T(8,128)S(1)}, f32[64,128]{1,0:T(8,128)S(1)}, f32[64,128,128]{2,1,0:T(8,128)S(1)}) fusion(f32[64,128,128]{2,1,0:T(8,128)S(1)} %multiply_reduce_fusion.11, f32[64,128]{1,0:T(8,128)S(1)} %bitcast.118, f32[64,128]{1,0:T(8,128)S(1)} %bitcast.115, f32[64,128,128]{2,1,0:T(8,128)S(1)} %fusion.72, ...), kind=kLoop, calls=%fused_computation.59.clone.1 | loop fusion | flops 38780928 | bytes 12845056 | tf_op jit(solution)/shard_map/while/body/eval_jaxpr/vmap()/reduce_sum | solution.py:37
  446.9 8.5 %multiply_reduce_fusion.12 = (f32[64,3,128]{2,1,0:T(4,128)S(1)}, f32[64,3,128]{2,1,0:T(4,128)S(1)}) fusion(f32[64,128,128]{2,1,0:T(8,128)S(1)} %get-tuple-element.365, f32[64,128,128]{2,1,0:T(8,128)S(1)} %add_sqrt_fusion.5, f32[64,3,128]{2,1,0:T(4,128)S(1)} %get-tuple-element.356, f32[64,3,128]{2,1,0:T(4,128)S(1)} %get-tuple-element.357), kind=kLoop, calls=%fused_computation.44.clone.1 | loop fusion | flops 15679488 | bytes 8781824 | tf_op jit(solution)/shard_map/while/body/eval_jaxpr/vmap()/reduce_sum | solution.py:37
  467.4 8.0 multiply_reduce_fusion.11
  475.6 9.2 %subtract_reduce_fusion.2 = (f32[64,128]{1,0:T(8,128)S(1)}, f32[64,128]{1,0:T(8,128)S(1)}, f32[64,128,128]{2,1,0:T(8,128)S(1)}) fusion(f32[64,128,128]{2,1,0:T(8,128)S(1)} %multiply_reduce_fusion.11, f32[64,128]{1,0:T(8,128)S(1)} %bitcast.118, f32[64,128]{1,0:T(8,128)S(1)} %bitcast.115, f32[64,128,128]{2,1,0:T(8,128)S(1)} %fusion.72, ...), kind=kLoop, calls=%fused_computation.59.clone.1 | loop fusion | flops 38780928 | bytes 12845056 | tf_op jit(solution)/shard_map/while/body/eval_jaxpr/vmap()/reduce_sum | solution.py:37
  484.8 8.5 %multiply_reduce_fusion.12 = (f32[64,3,128]{2,1,0:T(4,128)S(1)}, f32[64,3,128]{2,1,0:T(4,128)S(1)}) fusion(f32[64,128,128]{2,1,0:T(8,128)S(1)} %get-tuple-element.365, f32[64,128,128]{2,1,0:T(8,128)S(1)} %add_sqrt_fusion.5, f32[64,3,128]{2,1,0:T(4,128)S(1)} %get-tuple-element.356, f32[64,3,128]{2,1,0:T(4,128)S(1)} %get-tuple-element.357), kind=kLoop, calls=%fused_computation.44.clone.1 | loop fusion | flops 15679488 | bytes 8781824 | tf_op jit(solution)/shard_map/while/body/eval_jaxpr/vmap()/reduce_sum | solution.py:37
  505.3 8.0 multiply_reduce_fusion.11
  513.5 9.2 %subtract_reduce_fusion.2 = (f32[64,128]{1,0:T(8,128)S(1)}, f32[64,128]{1,0:T(8,128)S(1)}, f32[64,128,128]{2,1,0:T(8,128)S(1)}) fusion(f32[64,128,128]{2,1,0:T(8,128)S(1)} %multiply_reduce_fusion.11, f32[64,128]{1,0:T(8,128)S(1)} %bitcast.118, f32[64,128]{1,0:T(8,128)S(1)} %bitcast.115, f32[64,128,128]{2,1,0:T(8,128)S(1)} %fusion.72, ...), kind=kLoop, calls=%fused_computation.59.clone.1 | loop fusion | flops 38780928 | bytes 12845056 | tf_op jit(solution)/shard_map/while/body/eval_jaxpr/vmap()/reduce_sum | solution.py:37
  522.7 8.5 %multiply_reduce_fusion.12 = (f32[64,3,128]{2,1,0:T(4,128)S(1)}, f32[64,3,128]{2,1,0:T(4,128)S(1)}) fusion(f32[64,128,128]{2,1,0:T(8,128)S(1)} %get-tuple-element.365, f32[64,128,128]{2,1,0:T(8,128)S(1)} %add_sqrt_fusion.5, f32[64,3,128]{2,1,0:T(4,128)S(1)} %get-tuple-element.356, f32[64,3,128]{2,1,0:T(4,128)S(1)} %get-tuple-element.357), kind=kLoop, calls=%fused_computation.44.clone.1 | loop fusion | flops 15679488 | bytes 8781824 | tf_op jit(solution)/shard_map/while/body/eval_jaxpr/vmap()/reduce_sum | solution.py:37
  537.9 4.1 fusion.72
  543.2 8.0 multiply_reduce_fusion.11
  551.4 9.2 %subtract_reduce_fusion.2 = (f32[64,128]{1,0:T(8,128)S(1)}, f32[64,128]{1,0:T(8,128)S(1)}, f32[64,128,128]{2,1,0:T(8,128)S(1)}) fusion(f32[64,128,128]{2,1,0:T(8,128)S(1)} %multiply_reduce_fusion.11, f32[64,128]{1,0:T(8,128)S(1)} %bitcast.118, f32[64,128]{1,0:T(8,128)S(1)} %bitcast.115, f32[64,128,128]{2,1,0:T(8,128)S(1)} %fusion.72, ...), kind=kLoop, calls=%fused_computation.59.clone.1 | loop fusion | flops 38780928 | bytes 12845056 | tf_op jit(solution)/shard_map/while/body/eval_jaxpr/vmap()/reduce_sum | solution.py:37
  560.6 8.5 %multiply_reduce_fusion.12 = (f32[64,3,128]{2,1,0:T(4,128)S(1)}, f32[64,3,128]{2,1,0:T(4,128)S(1)}) fusion(f32[64,128,128]{2,1,0:T(8,128)S(1)} %get-tuple-element.365, f32[64,128,128]{2,1,0:T(8,128)S(1)} %add_sqrt_fusion.5, f32[64,3,128]{2,1,0:T(4,128)S(1)} %get-tuple-element.356, f32[64,3,128]{2,1,0:T(4,128)S(1)} %get-tuple-element.357), kind=kLoop, calls=%fused_computation.44.clone.1 | loop fusion | flops 15679488 | bytes 8781824 | tf_op jit(solution)/shard_map/while/body/eval_jaxpr/vmap()/reduce_sum | solution.py:37
  581.1 8.0 multiply_reduce_fusion.11
  589.2 9.2 %subtract_reduce_fusion.2 = (f32[64,128]{1,0:T(8,128)S(1)}, f32[64,128]{1,0:T(8,128)S(1)}, f32[64,128,128]{2,1,0:T(8,128)S(1)}) fusion(f32[64,128,128]{2,1,0:T(8,128)S(1)} %multiply_reduce_fusion.11, f32[64,128]{1,0:T(8,128)S(1)} %bitcast.118, f32[64,128]{1,0:T(8,128)S(1)} %bitcast.115, f32[64,128,128]{2,1,0:T(8,128)S(1)} %fusion.72, ...), kind=kLoop, calls=%fused_computation.59.clone.1 | loop fusion | flops 38780928 | bytes 12845056 | tf_op jit(solution)/shard_map/while/body/eval_jaxpr/vmap()/reduce_sum | solution.py:37
  598.4 8.5 %multiply_reduce_fusion.12 = (f32[64,3,128]{2,1,0:T(4,128)S(1)}, f32[64,3,128]{2,1,0:T(4,128)S(1)}) fusion(f32[64,128,128]{2,1,0:T(8,128)S(1)} %get-tuple-element.365, f32[64,128,128]{2,1,0:T(8,128)S(1)} %add_sqrt_fusion.5, f32[64,3,128]{2,1,0:T(4,128)S(1)} %get-tuple-element.356, f32[64,3,128]{2,1,0:T(4,128)S(1)} %get-tuple-element.357), kind=kLoop, calls=%fused_computation.44.clone.1 | loop fusion | flops 15679488 | bytes 8781824 | tf_op jit(solution)/shard_map/while/body/eval_jaxpr/vmap()/reduce_sum | solution.py:37
  618.9 8.0 multiply_reduce_fusion.11
  627.1 9.2 %subtract_reduce_fusion.2 = (f32[64,128]{1,0:T(8,128)S(1)}, f32[64,128]{1,0:T(8,128)S(1)}, f32[64,128,128]{2,1,0:T(8,128)S(1)}) fusion(f32[64,128,128]{2,1,0:T(8,128)S(1)} %multiply_reduce_fusion.11, f32[64,128]{1,0:T(8,128)S(1)} %bitcast.118, f32[64,128]{1,0:T(8,128)S(1)} %bitcast.115, f32[64,128,128]{2,1,0:T(8,128)S(1)} %fusion.72, ...), kind=kLoop, calls=%fused_computation.59.clone.1 | loop fusion | flops 38780928 | bytes 12845056 | tf_op jit(solution)/shard_map/while/body/eval_jaxpr/vmap()/reduce_sum | solution.py:37
  636.3 8.5 %multiply_reduce_fusion.12 = (f32[64,3,128]{2,1,0:T(4,128)S(1)}, f32[64,3,128]{2,1,0:T(4,128)S(1)}) fusion(f32[64,128,128]{2,1,0:T(8,128)S(1)} %get-tuple-element.365, f32[64,128,128]{2,1,0:T(8,128)S(1)} %add_sqrt_fusion.5, f32[64,3,128]{2,1,0:T(4,128)S(1)} %get-tuple-element.356, f32[64,3,128]{2,1,0:T(4,128)S(1)} %get-tuple-element.357), kind=kLoop, calls=%fused_computation.44.clone.1 | loop fusion | flops 15679488 | bytes 8781824 | tf_op jit(solution)/shard_map/while/body/eval_jaxpr/vmap()/reduce_sum | solution.py:37
  651.6 4.1 fusion.72
  656.8 8.0 multiply_reduce_fusion.11
  665.0 9.2 %subtract_reduce_fusion.2 = (f32[64,128]{1,0:T(8,128)S(1)}, f32[64,128]{1,0:T(8,128)S(1)}, f32[64,128,128]{2,1,0:T(8,128)S(1)}) fusion(f32[64,128,128]{2,1,0:T(8,128)S(1)} %multiply_reduce_fusion.11, f32[64,128]{1,0:T(8,128)S(1)} %bitcast.118, f32[64,128]{1,0:T(8,128)S(1)} %bitcast.115, f32[64,128,128]{2,1,0:T(8,128)S(1)} %fusion.72, ...), kind=kLoop, calls=%fused_computation.59.clone.1 | loop fusion | flops 38780928 | bytes 12845056 | tf_op jit(solution)/shard_map/while/body/eval_jaxpr/vmap()/reduce_sum | solution.py:37
  674.2 8.5 %multiply_reduce_fusion.12 = (f32[64,3,128]{2,1,0:T(4,128)S(1)}, f32[64,3,128]{2,1,0:T(4,128)S(1)}) fusion(f32[64,128,128]{2,1,0:T(8,128)S(1)} %get-tuple-element.365, f32[64,128,128]{2,1,0:T(8,128)S(1)} %add_sqrt_fusion.5, f32[64,3,128]{2,1,0:T(4,128)S(1)} %get-tuple-element.356, f32[64,3,128]{2,1,0:T(4,128)S(1)} %get-tuple-element.357), kind=kLoop, calls=%fused_computation.44.clone.1 | loop fusion | flops 15679488 | bytes 8781824 | tf_op jit(solution)/shard_map/while/body/eval_jaxpr/vmap()/reduce_sum | solution.py:37
  689.4 4.1 fusion.72
  694.7 8.0 multiply_reduce_fusion.11
  702.9 9.2 %subtract_reduce_fusion.2 = (f32[64,128]{1,0:T(8,128)S(1)}, f32[64,128]{1,0:T(8,128)S(1)}, f32[64,128,128]{2,1,0:T(8,128)S(1)}) fusion(f32[64,128,128]{2,1,0:T(8,128)S(1)} %multiply_reduce_fusion.11, f32[64,128]{1,0:T(8,128)S(1)} %bitcast.118, f32[64,128]{1,0:T(8,128)S(1)} %bitcast.115, f32[64,128,128]{2,1,0:T(8,128)S(1)} %fusion.72, ...), kind=kLoop, calls=%fused_computation.59.clone.1 | loop fusion | flops 38780928 | bytes 12845056 | tf_op jit(solution)/shard_map/while/body/eval_jaxpr/vmap()/reduce_sum | solution.py:37
  712.1 8.5 %multiply_reduce_fusion.12 = (f32[64,3,128]{2,1,0:T(4,128)S(1)}, f32[64,3,128]{2,1,0:T(4,128)S(1)}) fusion(f32[64,128,128]{2,1,0:T(8,128)S(1)} %get-tuple-element.365, f32[64,128,128]{2,1,0:T(8,128)S(1)} %add_sqrt_fusion.5, f32[64,3,128]{2,1,0:T(4,128)S(1)} %get-tuple-element.356, f32[64,3,128]{2,1,0:T(4,128)S(1)} %get-tuple-element.357), kind=kLoop, calls=%fused_computation.44.clone.1 | loop fusion | flops 15679488 | bytes 8781824 | tf_op jit(solution)/shard_map/while/body/eval_jaxpr/vmap()/reduce_sum | solution.py:37
  725.8 10.5 %collective-permute-done.1 = f32[192,512]{1,0:T(8,128)S(1)} collective-permute-done((f32[192,512]{1,0:T(8,128)S(1)}, f32[192,512]{1,0:T(8,128)S(1)}, u32[]{:S(2)}, u32[]{:S(2)}) %collective-permute-start.1) | collective-permute-done | bytes 393248 | tf_op jit(solution)/shard_map/ppermute | solution.py:15
  736.3 4.9 fusion.41
  741.3 69.2 %while.27 = (s32[]{:T(128)}, f32[8,16,4,128]{3,2,1,0:T(4,128)S(1)}, f32[8,16,9,128]{3,1,0,2:T(8,128)}, s32[]{:T(128)}) while((s32[]{:T(128)}, f32[8,16,4,128]{3,2,1,0:T(4,128)S(1)}, f32[8,16,9,128]{3,1,0,2:T(8,128)}, s32[]{:T(128)}) %tuple.104), condition=%wide.region_14.15_spmd, body=%wide.region_9.14_spmd.sunk | while | flops 18925568 | bytes 11239485 | solution.py:146
  810.5 14.3 %reduce-scatter.2.cloned.1.call-done = f32[128,512]{1,0:T(8,128)} async-done(((f32[2048,512]{1,0:T(8,128)}), f32[128,512]{1,0:T(8,128)}) %reduce-scatter.2.cloned.1.call-update) | async-done | bytes 262160 | tf_op jit(solution)/shard_map/reduce_scatter | solution.py:135
  (642 shorter events, 251.2 us)
Async XLA Ops:
  6.5 83.9 %all-gather.2.cloned.1.call-start = ((), (), s32[]{:S(2)}) async-start(), calls=%async_computation.1 | async-start | bytes 10027008 | tf_op jit(solution)/shard_map/all_gather | solution.py:95
  11.8 813.0 %reduce-scatter.2.cloned.1.call-start = ((), (), s32[]{:S(2)}) async-start(), calls=%async_computation.2 | async-start | bytes 4456448 | tf_op jit(solution)/shard_map/reduce_scatter | solution.py:135
  103.2 9.5 %copy-start.8 = (s32[1,1024,2]{1,2,0:T(2,128)S(1)}, s32[1,1024,2]{1,2,0:T(2,128)}, u32[]{:S(2)}) copy-start(s32[1,1024,2]{1,2,0:T(2,128)} %param.18) | copy-start | bytes 24580
  110.9 4.0 collective-permute-start
  117.3 3.2 copy-start.6
  143.9 8.6 %copy-start.5 = (s32[16,64]{1,0:T(8,128)S(1)}, s32[16,64]{1,0:T(8,128)}, u32[]{:S(2)}) copy-start(s32[16,64]{1,0:T(8,128)} %copy-done.4) | copy-start | bytes 12292 | tf_op jit(solution)/shard_map/while
  143.9 8.6 %copy-start.7 = (s32[16,64]{1,0:T(8,128)S(1)}, s32[16,64]{1,0:T(8,128)}, u32[]{:S(2)}) copy-start(s32[16,64]{1,0:T(8,128)} %copy-done.6) | copy-start | bytes 12292 | tf_op jit(solution)/shard_map/while
  143.9 10.1 %copy-start = (f32[192,512]{1,0:T(8,128)S(1)}, f32[192,512]{1,0:T(8,128)}, u32[]{:S(2)}) copy-start(f32[192,512]{1,0:T(8,128)} %get-tuple-element.382) | copy-start | bytes 1179652 | tf_op jit(solution)/shard_map/while
  155.2 3.2 copy-start.6
  181.7 8.6 %copy-start.5 = (s32[16,64]{1,0:T(8,128)S(1)}, s32[16,64]{1,0:T(8,128)}, u32[]{:S(2)}) copy-start(s32[16,64]{1,0:T(8,128)} %copy-done.4) | copy-start | bytes 12292 | tf_op jit(solution)/shard_map/while
  181.8 8.6 %copy-start.7 = (s32[16,64]{1,0:T(8,128)S(1)}, s32[16,64]{1,0:T(8,128)}, u32[]{:S(2)}) copy-start(s32[16,64]{1,0:T(8,128)} %copy-done.6) | copy-start | bytes 12292 | tf_op jit(solution)/shard_map/while
  181.8 10.1 %copy-start = (f32[192,512]{1,0:T(8,128)S(1)}, f32[192,512]{1,0:T(8,128)}, u32[]{:S(2)}) copy-start(f32[192,512]{1,0:T(8,128)} %get-tuple-element.382) | copy-start | bytes 1179652 | tf_op jit(solution)/shard_map/while
  193.1 3.2 copy-start.6
  219.6 8.6 %copy-start.5 = (s32[16,64]{1,0:T(8,128)S(1)}, s32[16,64]{1,0:T(8,128)}, u32[]{:S(2)}) copy-start(s32[16,64]{1,0:T(8,128)} %copy-done.4) | copy-start | bytes 12292 | tf_op jit(solution)/shard_map/while
  219.6 8.6 %copy-start.7 = (s32[16,64]{1,0:T(8,128)S(1)}, s32[16,64]{1,0:T(8,128)}, u32[]{:S(2)}) copy-start(s32[16,64]{1,0:T(8,128)} %copy-done.6) | copy-start | bytes 12292 | tf_op jit(solution)/shard_map/while
  219.6 10.1 %copy-start = (f32[192,512]{1,0:T(8,128)S(1)}, f32[192,512]{1,0:T(8,128)}, u32[]{:S(2)}) copy-start(f32[192,512]{1,0:T(8,128)} %get-tuple-element.382) | copy-start | bytes 1179652 | tf_op jit(solution)/shard_map/while
  231.0 3.2 copy-start.6
  257.5 8.6 %copy-start.5 = (s32[16,64]{1,0:T(8,128)S(1)}, s32[16,64]{1,0:T(8,128)}, u32[]{:S(2)}) copy-start(s32[16,64]{1,0:T(8,128)} %copy-done.4) | copy-start | bytes 12292 | tf_op jit(solution)/shard_map/while
  257.5 8.6 %copy-start.7 = (s32[16,64]{1,0:T(8,128)S(1)}, s32[16,64]{1,0:T(8,128)}, u32[]{:S(2)}) copy-start(s32[16,64]{1,0:T(8,128)} %copy-done.6) | copy-start | bytes 12292 | tf_op jit(solution)/shard_map/while
  257.5 10.1 %copy-start = (f32[192,512]{1,0:T(8,128)S(1)}, f32[192,512]{1,0:T(8,128)}, u32[]{:S(2)}) copy-start(f32[192,512]{1,0:T(8,128)} %get-tuple-element.382) | copy-start | bytes 1179652 | tf_op jit(solution)/shard_map/while
  268.9 3.2 copy-start.6
  295.4 8.6 %copy-start.5 = (s32[16,64]{1,0:T(8,128)S(1)}, s32[16,64]{1,0:T(8,128)}, u32[]{:S(2)}) copy-start(s32[16,64]{1,0:T(8,128)} %copy-done.4) | copy-start | bytes 12292 | tf_op jit(solution)/shard_map/while
  295.4 8.6 %copy-start.7 = (s32[16,64]{1,0:T(8,128)S(1)}, s32[16,64]{1,0:T(8,128)}, u32[]{:S(2)}) copy-start(s32[16,64]{1,0:T(8,128)} %copy-done.6) | copy-start | bytes 12292 | tf_op jit(solution)/shard_map/while
  295.4 10.1 %copy-start = (f32[192,512]{1,0:T(8,128)S(1)}, f32[192,512]{1,0:T(8,128)}, u32[]{:S(2)}) copy-start(f32[192,512]{1,0:T(8,128)} %get-tuple-element.382) | copy-start | bytes 1179652 | tf_op jit(solution)/shard_map/while
  306.7 3.2 copy-start.6
  333.3 8.6 %copy-start.5 = (s32[16,64]{1,0:T(8,128)S(1)}, s32[16,64]{1,0:T(8,128)}, u32[]{:S(2)}) copy-start(s32[16,64]{1,0:T(8,128)} %copy-done.4) | copy-start | bytes 12292 | tf_op jit(solution)/shard_map/while
  333.3 8.6 %copy-start.7 = (s32[16,64]{1,0:T(8,128)S(1)}, s32[16,64]{1,0:T(8,128)}, u32[]{:S(2)}) copy-start(s32[16,64]{1,0:T(8,128)} %copy-done.6) | copy-start | bytes 12292 | tf_op jit(solution)/shard_map/while
  333.3 10.1 %copy-start = (f32[192,512]{1,0:T(8,128)S(1)}, f32[192,512]{1,0:T(8,128)}, u32[]{:S(2)}) copy-start(f32[192,512]{1,0:T(8,128)} %get-tuple-element.382) | copy-start | bytes 1179652 | tf_op jit(solution)/shard_map/while
  344.6 3.2 copy-start.6
  371.1 8.6 %copy-start.5 = (s32[16,64]{1,0:T(8,128)S(1)}, s32[16,64]{1,0:T(8,128)}, u32[]{:S(2)}) copy-start(s32[16,64]{1,0:T(8,128)} %copy-done.4) | copy-start | bytes 12292 | tf_op jit(solution)/shard_map/while
  371.2 8.6 %copy-start.7 = (s32[16,64]{1,0:T(8,128)S(1)}, s32[16,64]{1,0:T(8,128)}, u32[]{:S(2)}) copy-start(s32[16,64]{1,0:T(8,128)} %copy-done.6) | copy-start | bytes 12292 | tf_op jit(solution)/shard_map/while
  371.2 10.1 %copy-start = (f32[192,512]{1,0:T(8,128)S(1)}, f32[192,512]{1,0:T(8,128)}, u32[]{:S(2)}) copy-start(f32[192,512]{1,0:T(8,128)} %get-tuple-element.382) | copy-start | bytes 1179652 | tf_op jit(solution)/shard_map/while
  382.5 3.2 copy-start.6
  409.0 8.6 %copy-start.5 = (s32[16,64]{1,0:T(8,128)S(1)}, s32[16,64]{1,0:T(8,128)}, u32[]{:S(2)}) copy-start(s32[16,64]{1,0:T(8,128)} %copy-done.4) | copy-start | bytes 12292 | tf_op jit(solution)/shard_map/while
  409.0 8.6 %copy-start.7 = (s32[16,64]{1,0:T(8,128)S(1)}, s32[16,64]{1,0:T(8,128)}, u32[]{:S(2)}) copy-start(s32[16,64]{1,0:T(8,128)} %copy-done.6) | copy-start | bytes 12292 | tf_op jit(solution)/shard_map/while
  409.0 10.1 %copy-start = (f32[192,512]{1,0:T(8,128)S(1)}, f32[192,512]{1,0:T(8,128)}, u32[]{:S(2)}) copy-start(f32[192,512]{1,0:T(8,128)} %get-tuple-element.382) | copy-start | bytes 1179652 | tf_op jit(solution)/shard_map/while
  420.4 3.2 copy-start.6
  446.9 8.6 %copy-start.5 = (s32[16,64]{1,0:T(8,128)S(1)}, s32[16,64]{1,0:T(8,128)}, u32[]{:S(2)}) copy-start(s32[16,64]{1,0:T(8,128)} %copy-done.4) | copy-start | bytes 12292 | tf_op jit(solution)/shard_map/while
  446.9 8.6 %copy-start.7 = (s32[16,64]{1,0:T(8,128)S(1)}, s32[16,64]{1,0:T(8,128)}, u32[]{:S(2)}) copy-start(s32[16,64]{1,0:T(8,128)} %copy-done.6) | copy-start | bytes 12292 | tf_op jit(solution)/shard_map/while
  446.9 10.1 %copy-start = (f32[192,512]{1,0:T(8,128)S(1)}, f32[192,512]{1,0:T(8,128)}, u32[]{:S(2)}) copy-start(f32[192,512]{1,0:T(8,128)} %get-tuple-element.382) | copy-start | bytes 1179652 | tf_op jit(solution)/shard_map/while
  458.3 3.2 copy-start.6
  484.8 8.6 %copy-start.5 = (s32[16,64]{1,0:T(8,128)S(1)}, s32[16,64]{1,0:T(8,128)}, u32[]{:S(2)}) copy-start(s32[16,64]{1,0:T(8,128)} %copy-done.4) | copy-start | bytes 12292 | tf_op jit(solution)/shard_map/while
  484.8 8.6 %copy-start.7 = (s32[16,64]{1,0:T(8,128)S(1)}, s32[16,64]{1,0:T(8,128)}, u32[]{:S(2)}) copy-start(s32[16,64]{1,0:T(8,128)} %copy-done.6) | copy-start | bytes 12292 | tf_op jit(solution)/shard_map/while
  484.8 10.1 %copy-start = (f32[192,512]{1,0:T(8,128)S(1)}, f32[192,512]{1,0:T(8,128)}, u32[]{:S(2)}) copy-start(f32[192,512]{1,0:T(8,128)} %get-tuple-element.382) | copy-start | bytes 1179652 | tf_op jit(solution)/shard_map/while
  522.7 8.6 %copy-start.5 = (s32[16,64]{1,0:T(8,128)S(1)}, s32[16,64]{1,0:T(8,128)}, u32[]{:S(2)}) copy-start(s32[16,64]{1,0:T(8,128)} %copy-done.4) | copy-start | bytes 12292 | tf_op jit(solution)/shard_map/while
  522.7 8.6 %copy-start.7 = (s32[16,64]{1,0:T(8,128)S(1)}, s32[16,64]{1,0:T(8,128)}, u32[]{:S(2)}) copy-start(s32[16,64]{1,0:T(8,128)} %copy-done.6) | copy-start | bytes 12292 | tf_op jit(solution)/shard_map/while
  522.7 10.1 %copy-start = (f32[192,512]{1,0:T(8,128)S(1)}, f32[192,512]{1,0:T(8,128)}, u32[]{:S(2)}) copy-start(f32[192,512]{1,0:T(8,128)} %get-tuple-element.382) | copy-start | bytes 1179652 | tf_op jit(solution)/shard_map/while
  560.5 8.6 %copy-start.5 = (s32[16,64]{1,0:T(8,128)S(1)}, s32[16,64]{1,0:T(8,128)}, u32[]{:S(2)}) copy-start(s32[16,64]{1,0:T(8,128)} %copy-done.4) | copy-start | bytes 12292 | tf_op jit(solution)/shard_map/while
  560.6 8.6 %copy-start.7 = (s32[16,64]{1,0:T(8,128)S(1)}, s32[16,64]{1,0:T(8,128)}, u32[]{:S(2)}) copy-start(s32[16,64]{1,0:T(8,128)} %copy-done.6) | copy-start | bytes 12292 | tf_op jit(solution)/shard_map/while
  560.6 10.1 %copy-start = (f32[192,512]{1,0:T(8,128)S(1)}, f32[192,512]{1,0:T(8,128)}, u32[]{:S(2)}) copy-start(f32[192,512]{1,0:T(8,128)} %get-tuple-element.382) | copy-start | bytes 1179652 | tf_op jit(solution)/shard_map/while
  571.9 3.2 copy-start.6
  598.4 8.6 %copy-start.5 = (s32[16,64]{1,0:T(8,128)S(1)}, s32[16,64]{1,0:T(8,128)}, u32[]{:S(2)}) copy-start(s32[16,64]{1,0:T(8,128)} %copy-done.4) | copy-start | bytes 12292 | tf_op jit(solution)/shard_map/while
  598.4 8.6 %copy-start.7 = (s32[16,64]{1,0:T(8,128)S(1)}, s32[16,64]{1,0:T(8,128)}, u32[]{:S(2)}) copy-start(s32[16,64]{1,0:T(8,128)} %copy-done.6) | copy-start | bytes 12292 | tf_op jit(solution)/shard_map/while
  598.4 10.1 %copy-start = (f32[192,512]{1,0:T(8,128)S(1)}, f32[192,512]{1,0:T(8,128)}, u32[]{:S(2)}) copy-start(f32[192,512]{1,0:T(8,128)} %get-tuple-element.382) | copy-start | bytes 1179652 | tf_op jit(solution)/shard_map/while
  636.3 8.6 %copy-start.5 = (s32[16,64]{1,0:T(8,128)S(1)}, s32[16,64]{1,0:T(8,128)}, u32[]{:S(2)}) copy-start(s32[16,64]{1,0:T(8,128)} %copy-done.4) | copy-start | bytes 12292 | tf_op jit(solution)/shard_map/while
  636.3 8.6 %copy-start.7 = (s32[16,64]{1,0:T(8,128)S(1)}, s32[16,64]{1,0:T(8,128)}, u32[]{:S(2)}) copy-start(s32[16,64]{1,0:T(8,128)} %copy-done.6) | copy-start | bytes 12292 | tf_op jit(solution)/shard_map/while
  636.3 10.1 %copy-start = (f32[192,512]{1,0:T(8,128)S(1)}, f32[192,512]{1,0:T(8,128)}, u32[]{:S(2)}) copy-start(f32[192,512]{1,0:T(8,128)} %get-tuple-element.382) | copy-start | bytes 1179652 | tf_op jit(solution)/shard_map/while
  674.2 8.6 %copy-start.5 = (s32[16,64]{1,0:T(8,128)S(1)}, s32[16,64]{1,0:T(8,128)}, u32[]{:S(2)}) copy-start(s32[16,64]{1,0:T(8,128)} %copy-done.4) | copy-start | bytes 12292 | tf_op jit(solution)/shard_map/while
  674.2 8.6 %copy-start.7 = (s32[16,64]{1,0:T(8,128)S(1)}, s32[16,64]{1,0:T(8,128)}, u32[]{:S(2)}) copy-start(s32[16,64]{1,0:T(8,128)} %copy-done.6) | copy-start | bytes 12292 | tf_op jit(solution)/shard_map/while
  674.2 10.1 %copy-start = (f32[192,512]{1,0:T(8,128)S(1)}, f32[192,512]{1,0:T(8,128)}, u32[]{:S(2)}) copy-start(f32[192,512]{1,0:T(8,128)} %get-tuple-element.382) | copy-start | bytes 1179652 | tf_op jit(solution)/shard_map/while
  712.1 8.6 %copy-start.5 = (s32[16,64]{1,0:T(8,128)S(1)}, s32[16,64]{1,0:T(8,128)}, u32[]{:S(2)}) copy-start(s32[16,64]{1,0:T(8,128)} %copy-done.4) | copy-start | bytes 12292 | tf_op jit(solution)/shard_map/while
  712.1 8.6 %copy-start.7 = (s32[16,64]{1,0:T(8,128)S(1)}, s32[16,64]{1,0:T(8,128)}, u32[]{:S(2)}) copy-start(s32[16,64]{1,0:T(8,128)} %copy-done.6) | copy-start | bytes 12292 | tf_op jit(solution)/shard_map/while
  712.1 10.1 %copy-start = (f32[192,512]{1,0:T(8,128)S(1)}, f32[192,512]{1,0:T(8,128)}, u32[]{:S(2)}) copy-start(f32[192,512]{1,0:T(8,128)} %get-tuple-element.382) | copy-start | bytes 1179652 | tf_op jit(solution)/shard_map/while
  723.4 12.9 %collective-permute-start.1 = (f32[192,512]{1,0:T(8,128)S(1)}, f32[192,512]{1,0:T(8,128)S(1)}, u32[]{:S(2)}, u32[]{:S(2)}) collective-permute-start(f32[192,512]{1,0:T(8,128)S(1)} %slice.109), channel_id=1, source_target_pairs={{16,0},{32,16},{48,32},{64,48},{80,64},{96,80},{112,96},{17,1},{33... | collective-permute-start | bytes 1179656 | tf_op jit(solution)/shard_map/ppermute | solution.py:15
  (54 other events, 98.3 us)
Sparse Core Ops, SparseCore 0:
  12.0 78.4 all-gather.1
  741.4 83.3 reduce-scatter.1
where the time goes:
time: 836 us; the launch traced here: 833 us
  other arithmetic  564 us (67%)
  local copies, waits for them, and re-layouts  123 us (15%)
  waiting for transfers between devices  76 us (9%)
  blocking collectives  25.4 us (3%)
  matrix products  23.4 us (3%)
  between operations  14.2 us (2%)
    reduce_sum x16, other arithmetic, tile_pair(): jnp.sum(viscous - conduct, 0)[None]  147 us
    reduce_sum x16, other arithmetic, tile_pair(): jnp.sum(force, 1)  135 us
    reduce_sum x16, other arithmetic, tile_pair(): along = jnp.sum(unit * relative, 0)  128 us
    reduce_sum x16, other arithmetic, tile_pair(): radius = jnp.sqrt(jnp.sum(offset * offset, 0) + 0.01)  66.2 us
    all_gather x1, waiting for transfers between devices, per_device(): group_data = lax.all_gather(owned, 'tile', axis=0, tiled=True)  50.3 us
    gather x16, local copies, waits for them, and re-layouts, consume(): reachable[second_index]  39.7 us
    all_gather x1, blocking collectives, per_device(): tables = lax.all_gather(exported_tile_places, 'tile', axis=0, tiled=True)  25.4 us
    mul x8, other arithmetic, tile_self(): (repulse * weight - friction * weight * weight * along + noise_amp * weig...  19.2 us
  transfers between devices with their start and end apart: 4, of which 4 were waited for; matrix products, arithmetic and copies ran while one was open for 9% of the time, Pallas kernels for 0%

commit v1 on v0

--- a/solution.py
+++ b/solution.py
@@ -92,7 +92,10 @@
         0,
     )
     owned = owned.reshape(9, blocks, 128).transpose(1, 0, 2)
-    group_data = lax.all_gather(owned, "tile", axis=0, tiled=True)
+    devices = lax.axis_size("tile")
+    pieces = jnp.stack([owned for _ in range(devices)])
+    pieces = lax.all_to_all(pieces, "tile", split_axis=0, concat_axis=0)
+    group_data = jnp.concatenate(pieces, axis=0)
     tables = lax.all_gather(exported_tile_places, "tile", axis=0, tiled=True)
     my_index = lax.axis_index("tile")
     my_slots = lax.dynamic_index_in_dim(tables, my_index, 1, keepdims=False)

time: 836 us -> 972 us (1.16)
  blocking collectives: 25.4 us -> 186 us
  waiting for transfers between devices: 76 us -> 25.6 us
  local copies, waits for them, and re-layouts: 123 us -> 141 us
    all_gather x1, blocking collectives: 25.4 us -> 186 us  [per_device(): tables = lax.all_gather(exported_tile_places, 'tile', axis=0, tiled=True)]
    all_gather x1 -> x0, waiting for transfers between devices: 50.3 us -> none  [per_device(): group_data = lax.all_gather(owned, 'tile', axis=0, tiled=True)]
    reshape x0 -> x1, local copies, waits for them, and re-layouts: none -> 22.5 us  [per_device(): group_data = jnp.concatenate(pieces, axis=0)]
    all_gather x1 -> x0, local copies, waits for them, and re-layouts: 12.8 us -> none  [per_device(): group_data = lax.all_gather(owned, 'tile', axis=0, tiled=True)]
  transfers between devices with their start and end apart: 4 -> 4, of which waited for: 4 -> 3; matrix products, arithmetic and copies ran while one was open for 9% -> 7% of each run, Pallas kernels for 0% -> 0%
where the time goes in v1:
time: 972 us; the launch traced here: 970 us
  other arithmetic  564 us (58%)
  blocking collectives  186 us (19%)
  local copies, waits for them, and re-layouts  141 us (15%)
  waiting for transfers between devices  25.6 us (3%)
  matrix products  23.4 us (2%)
  between operations  14.2 us (1%)
  starting transfers between devices  11.4 us (1%)
    all_gather x1, blocking collectives, per_device(): tables = lax.all_gather(exported_tile_places, 'tile', axis=0, tiled=True)  186 us
    reduce_sum x16, other arithmetic, tile_pair(): jnp.sum(viscous - conduct, 0)[None]  147 us
    reduce_sum x16, other arithmetic, tile_pair(): jnp.sum(force, 1)  135 us
    reduce_sum x16, other arithmetic, tile_pair(): along = jnp.sum(unit * relative, 0)  128 us
    reduce_sum x16, other arithmetic, tile_pair(): radius = jnp.sqrt(jnp.sum(offset * offset, 0) + 0.01)  66.2 us
    gather x16, local copies, waits for them, and re-layouts, consume(): reachable[second_index]  39.7 us
    reshape x1, local copies, waits for them, and re-layouts, per_device(): group_data = jnp.concatenate(pieces, axis=0)  22.5 us
  transfers between devices with their start and end apart: 4, of which 3 were waited for; matrix products, arithmetic and copies ran while one was open for 7% of the time, Pallas kernels for 0%

profile of v1, /device:TPU:0, one launch (start us, length us, event | category | flops | bytes accessed | tf_op | source)
XLA Modules:
  0.0 969.7 jit_solution(10995851649398289915)
XLA Ops:
  11.8 4.8 stack.2
  16.7 8.3 all-to-all-start
  25.1 185.6 %all_gather.3 = s32[16,16,12]{2,1,0:T(8,128)S(1)} all-gather(s32[1,16,12]{2,1,0:T(8,128)S(1)} %copy.43), channel_id=1, replica_groups=mesh['grp'=8,'tile'=16] {'tile'}, dimensions={0}, use_global_device_ids=true | all-gather | bytes 13056 | tf_op jit(solution)/shard_map/all_gather | solution.py:99
  212.8 4.4 copy.44
  217.2 22.5 %copy.45 = f32[2048,9,128]{2,1,0:T(8,128)} copy(f32[2048,9,128]{2,0,1:T(8,128)S(1)} %bitcast.110) | data formatting | bytes 18874368 | tf_op jit(solution)/shard_map/reshape | solution.py:98
  239.7 6.5 gather_fusion.2
  253.4 606.1 %while.28 = (s32[]{:T(128)}, f32[192,512]{1,0:T(8,128)}, f32[384,512]{1,0:T(8,128)S(1)}, s32[16,64]{1,0:T(8,128)S(1)}, f32[192,9,128]{2,1,0:T(8,128)S(1)}, /*ind...) while((s32[]{:T(128)}, f32[192,512]{1,0:T(8,128)}, ...), condition=%wide.region_7.8_spmd.clone, body=%wide.region_0.7_spmd.clone.sunk | while | flops 305871232 | bytes 52507452 | solution.py:134
  262.5 8.0 multiply_reduce_fusion.11
  270.7 9.2 subtract_reduce_fusion.2
  279.9 8.5 multiply_reduce_fusion.12
  300.4 8.0 multiply_reduce_fusion.11
  308.6 9.2 subtract_reduce_fusion.2
  317.8 8.5 multiply_reduce_fusion.12
  338.3 8.0 multiply_reduce_fusion.11
  346.5 9.2 subtract_reduce_fusion.2
  355.7 8.5 multiply_reduce_fusion.12
  376.2 8.0 multiply_reduce_fusion.11
  384.4 9.2 subtract_reduce_fusion.2
  393.6 8.5 multiply_reduce_fusion.12
  414.1 8.0 multiply_reduce_fusion.11
  422.2 9.2 subtract_reduce_fusion.2
  431.4 8.5 multiply_reduce_fusion.12
  446.7 4.1 fusion.72
  451.9 8.0 multiply_reduce_fusion.11
  460.1 9.2 subtract_reduce_fusion.2
  469.3 8.5 multiply_reduce_fusion.12
  484.6 4.1 fusion.72
  489.8 8.0 multiply_reduce_fusion.11
  498.0 9.2 subtract_reduce_fusion.2
  507.2 8.5 multiply_reduce_fusion.12
  527.7 8.0 multiply_reduce_fusion.11
  535.9 9.2 subtract_reduce_fusion.2
  545.1 8.5 multiply_reduce_fusion.12
  565.6 8.0 multiply_reduce_fusion.11
  573.8 9.2 subtract_reduce_fusion.2
  583.0 8.5 multiply_reduce_fusion.12
  598.2 4.1 fusion.72
  603.5 8.0 multiply_reduce_fusion.11
  611.6 9.2 subtract_reduce_fusion.2
  620.8 8.5 multiply_reduce_fusion.12
  636.1 4.1 fusion.72
  641.3 8.0 multiply_reduce_fusion.11
  649.5 9.2 subtract_reduce_fusion.2
  658.7 8.5 multiply_reduce_fusion.12
  674.0 4.1 fusion.72
  679.2 8.0 multiply_reduce_fusion.11
  687.4 9.2 subtract_reduce_fusion.2
  696.6 8.5 multiply_reduce_fusion.12
  717.1 8.0 multiply_reduce_fusion.11
  725.3 9.2 subtract_reduce_fusion.2
  734.5 8.5 multiply_reduce_fusion.12
  755.0 8.0 multiply_reduce_fusion.11
  763.2 9.2 subtract_reduce_fusion.2
  772.4 8.5 multiply_reduce_fusion.12
  792.9 8.0 multiply_reduce_fusion.11
  801.0 9.2 subtract_reduce_fusion.2
  810.2 8.5 multiply_reduce_fusion.12
  830.7 8.0 multiply_reduce_fusion.11
  838.9 9.2 subtract_reduce_fusion.2
  848.1 8.5 multiply_reduce_fusion.12
  861.9 11.0 %collective-permute-done.1 = f32[192,512]{1,0:T(8,128)S(1)} collective-permute-done((f32[192,512]{1,0:T(8,128)S(1)}, f32[192,512]{1,0:T(8,128)S(1)}, u32[]{:S(2)}, u32[]{:S(2)}) %collective-permute-start.1) | collective-permute-done | bytes 393248 | tf_op jit(solution)/shard_map/ppermute | solution.py:15
  872.8 4.9 fusion.41
  877.8 69.2 %while.27 = (s32[]{:T(128)}, f32[8,16,4,128]{3,2,1,0:T(4,128)S(1)}, f32[8,16,9,128]{3,1,0,2:T(8,128)}, s32[]{:T(128)}) while((s32[]{:T(128)}, f32[8,16,4,128]{3,2,1,0:T(4,128)S(1)}, f32[8,16,9,128]{3,1,0,2:T(8,128)}, s32[]{:T(128)}) %tuple.100), condition=%wide.region_14.15_spmd, body=%wide.region_9.14_spmd.sunk | while | flops 18925568 | bytes 11239485 | solution.py:149
  947.0 14.0 %reduce-scatter.2.cloned.1.call-done = f32[128,512]{1,0:T(8,128)} async-done(((f32[2048,512]{1,0:T(8,128)}), f32[128,512]{1,0:T(8,128)}) %reduce-scatter.2.cloned.1.call-update) | async-done | bytes 262160 | tf_op jit(solution)/shard_map/reduce_scatter | solution.py:138
  (645 shorter events, 258.3 us)
Async XLA Ops:
  16.7 8.4 copy-start.9
  16.7 196.1 %all-to-all-start = ((f32[16,128,9,128]{3,1,2,0:T(8,128)}), f32[16,128,9,128]{3,1,2,0:T(8,128)}, u32[]{:S(2)}, u32[]{:S(2)}) async-start(f32[16,128,9,128]{3,1,2,0:T(8,128)} %stack.2), calls=%async_computation | async-start | bytes 18874368 | tf_op jit(solution)/shard_map/all_to_all | solution.py:97
  25.0 936.1 %reduce-scatter.2.cloned.1.call-start = ((), (), s32[]{:S(2)}) async-start(), calls=%async_computation.2 | async-start | bytes 4456448 | tf_op jit(solution)/shard_map/reduce_scatter | solution.py:138
  239.7 9.2 copy-start.8
  247.4 3.5 collective-permute-start
  253.4 3.2 copy-start.6
  279.9 8.6 copy-start.5
  279.9 8.6 copy-start.7
  279.9 10.1 %copy-start = (f32[192,512]{1,0:T(8,128)S(1)}, f32[192,512]{1,0:T(8,128)}, u32[]{:S(2)}) copy-start(f32[192,512]{1,0:T(8,128)} %get-tuple-element.376) | copy-start | bytes 1179652 | tf_op jit(solution)/shard_map/while
  291.2 3.2 copy-start.6
  317.8 8.6 copy-start.5
  317.8 8.6 copy-start.7
  317.8 10.1 %copy-start = (f32[192,512]{1,0:T(8,128)S(1)}, f32[192,512]{1,0:T(8,128)}, u32[]{:S(2)}) copy-start(f32[192,512]{1,0:T(8,128)} %get-tuple-element.376) | copy-start | bytes 1179652 | tf_op jit(solution)/shard_map/while
  329.1 3.2 copy-start.6
  355.7 8.6 copy-start.5
  355.7 8.6 copy-start.7
  355.7 10.1 %copy-start = (f32[192,512]{1,0:T(8,128)S(1)}, f32[192,512]{1,0:T(8,128)}, u32[]{:S(2)}) copy-start(f32[192,512]{1,0:T(8,128)} %get-tuple-element.376) | copy-start | bytes 1179652 | tf_op jit(solution)/shard_map/while
  367.0 3.2 copy-start.6
  393.5 8.6 copy-start.5
  393.5 8.6 copy-start.7
  393.6 10.1 %copy-start = (f32[192,512]{1,0:T(8,128)S(1)}, f32[192,512]{1,0:T(8,128)}, u32[]{:S(2)}) copy-start(f32[192,512]{1,0:T(8,128)} %get-tuple-element.376) | copy-start | bytes 1179652 | tf_op jit(solution)/shard_map/while
  404.9 3.2 copy-start.6
  431.4 8.6 copy-start.5
  431.4 8.6 copy-start.7
  431.4 10.1 %copy-start = (f32[192,512]{1,0:T(8,128)S(1)}, f32[192,512]{1,0:T(8,128)}, u32[]{:S(2)}) copy-start(f32[192,512]{1,0:T(8,128)} %get-tuple-element.376) | copy-start | bytes 1179652 | tf_op jit(solution)/shard_map/while
  442.8 3.2 copy-start.6
  469.3 8.6 copy-start.5
  469.3 8.6 copy-start.7
  469.3 10.1 %copy-start = (f32[192,512]{1,0:T(8,128)S(1)}, f32[192,512]{1,0:T(8,128)}, u32[]{:S(2)}) copy-start(f32[192,512]{1,0:T(8,128)} %get-tuple-element.376) | copy-start | bytes 1179652 | tf_op jit(solution)/shard_map/while
  480.6 3.2 copy-start.6
  507.2 8.6 copy-start.5
  507.2 8.6 copy-start.7
  507.2 10.1 %copy-start = (f32[192,512]{1,0:T(8,128)S(1)}, f32[192,512]{1,0:T(8,128)}, u32[]{:S(2)}) copy-start(f32[192,512]{1,0:T(8,128)} %get-tuple-element.376) | copy-start | bytes 1179652 | tf_op jit(solution)/shard_map/while
  518.5 3.2 copy-start.6
  545.1 8.6 copy-start.5
  545.1 8.6 copy-start.7
  545.1 10.1 %copy-start = (f32[192,512]{1,0:T(8,128)S(1)}, f32[192,512]{1,0:T(8,128)}, u32[]{:S(2)}) copy-start(f32[192,512]{1,0:T(8,128)} %get-tuple-element.376) | copy-start | bytes 1179652 | tf_op jit(solution)/shard_map/while
  556.4 3.2 copy-start.6
  582.9 8.6 copy-start.5
  582.9 8.6 copy-start.7
  583.0 10.1 %copy-start = (f32[192,512]{1,0:T(8,128)S(1)}, f32[192,512]{1,0:T(8,128)}, u32[]{:S(2)}) copy-start(f32[192,512]{1,0:T(8,128)} %get-tuple-element.376) | copy-start | bytes 1179652 | tf_op jit(solution)/shard_map/while
  594.3 3.2 copy-start.6
  620.8 8.6 copy-start.5
  620.8 8.6 copy-start.7
  620.8 10.1 %copy-start = (f32[192,512]{1,0:T(8,128)S(1)}, f32[192,512]{1,0:T(8,128)}, u32[]{:S(2)}) copy-start(f32[192,512]{1,0:T(8,128)} %get-tuple-element.376) | copy-start | bytes 1179652 | tf_op jit(solution)/shard_map/while
  658.7 8.6 copy-start.5
  658.7 8.6 copy-start.7
  658.7 10.1 %copy-start = (f32[192,512]{1,0:T(8,128)S(1)}, f32[192,512]{1,0:T(8,128)}, u32[]{:S(2)}) copy-start(f32[192,512]{1,0:T(8,128)} %get-tuple-element.376) | copy-start | bytes 1179652 | tf_op jit(solution)/shard_map/while
  696.6 8.6 copy-start.5
  696.6 8.6 copy-start.7
  696.6 10.1 %copy-start = (f32[192,512]{1,0:T(8,128)S(1)}, f32[192,512]{1,0:T(8,128)}, u32[]{:S(2)}) copy-start(f32[192,512]{1,0:T(8,128)} %get-tuple-element.376) | copy-start | bytes 1179652 | tf_op jit(solution)/shard_map/while
  734.5 8.6 copy-start.5
  734.5 8.6 copy-start.7
  734.5 10.1 %copy-start = (f32[192,512]{1,0:T(8,128)S(1)}, f32[192,512]{1,0:T(8,128)}, u32[]{:S(2)}) copy-start(f32[192,512]{1,0:T(8,128)} %get-tuple-element.376) | copy-start | bytes 1179652 | tf_op jit(solution)/shard_map/while
  772.3 8.6 copy-start.5
  772.3 8.6 copy-start.7
  772.4 10.1 %copy-start = (f32[192,512]{1,0:T(8,128)S(1)}, f32[192,512]{1,0:T(8,128)}, u32[]{:S(2)}) copy-start(f32[192,512]{1,0:T(8,128)} %get-tuple-element.376) | copy-start | bytes 1179652 | tf_op jit(solution)/shard_map/while
  810.2 8.6 copy-start.5
  810.2 8.6 copy-start.7
  810.2 10.1 %copy-start = (f32[192,512]{1,0:T(8,128)S(1)}, f32[192,512]{1,0:T(8,128)}, u32[]{:S(2)}) copy-start(f32[192,512]{1,0:T(8,128)} %get-tuple-element.376) | copy-start | bytes 1179652 | tf_op jit(solution)/shard_map/while
  848.1 8.6 copy-start.5
  848.1 8.6 copy-start.7
  848.1 10.1 %copy-start = (f32[192,512]{1,0:T(8,128)S(1)}, f32[192,512]{1,0:T(8,128)}, u32[]{:S(2)}) copy-start(f32[192,512]{1,0:T(8,128)} %get-tuple-element.376) | copy-start | bytes 1179652 | tf_op jit(solution)/shard_map/while
  859.5 13.4 %collective-permute-start.1 = (f32[192,512]{1,0:T(8,128)S(1)}, f32[192,512]{1,0:T(8,128)S(1)}, u32[]{:S(2)}, u32[]{:S(2)}) collective-permute-start(f32[192,512]{1,0:T(8,128)S(1)} %slice.109), channel_id=1, source_target_pairs={{16,0},{32,16},{48,32},{64,48},{80,64},{96,80},{112,96},{17,1},{33... | collective-permute-start | bytes 1179656 | tf_op jit(solution)/shard_map/ppermute | solution.py:15
  (55 other events, 101.6 us)
Sparse Core Ops, SparseCore 0:
  877.9 83.1 reduce-scatter.1
